TPU v7x, 32 devices: a whole 2x2x4 slice. The times are simulated.
32 devices in a mesh: blk: 1, dev: 32 (over z, y, x, core).
Axes of the slice: x: 2, y: 2, z: 4, core: 2. Of those that a mesh axis runs over, the one named last changes fastest.
Arguments:
- echoes: bfloat16 [2, 4, 256, 16384], P(None, None, ('blk', 'dev')), may hold values from -6 to 6
- range_phase: float32 [16384], replicated, may hold values from -3.140625 to 3.140625
- offsets: int32 [16384], P('dev'), may hold values from 0 to 56, as said below
- tap_weights: float32 [8, 384], replicated, may hold values from -2 to 2
- channel_mix: float32 [2, 4, 4, 384], replicated, may hold values from -2 to 2
- azimuth_filter: float32 [2, 4, 384], replicated, may hold values from -4 to 4
Outputs:
- focused_image: bfloat16 [2, 4, 256, 16384], P(None, None, 'blk', 'dev')
Inputs may be any that keep to these rules, and one draw needn't show every extreme that they name: `offsets`: each range bin's offset lies between 0 and 56; some range bin has exactly 56.
All inputs are finite; a program needn't handle non-finite values.
Results may differ from a plain program's by a relative error of at most 0.0088.
Values may be sent and summed in bfloat16 or wider, within the bound.
A program may use at most 128 MiB of HBM per device.

v0:
```python
import math

import jax
import jax.numpy as jnp
from jax import lax
from jax.sharding import PartitionSpec as P

R1 = 128
MARG = 64


def shifted(block, axis, distance):
    devices = range(lax.axis_size(axis))
    route = [(i - distance, i) for i in devices if i - distance in devices]
    return lax.ppermute(block, axis, route)


def phase_pair(row_count, col_count, length, direction, factor):
    product = (
        jnp.arange(row_count, dtype=jnp.int32)[:, None]
        * jnp.arange(col_count, dtype=jnp.int32)[None, :]
        % length
    )
    angle = product.astype(jnp.float32) * (direction * 2.0 * math.pi / length)
    return (jnp.cos(angle) * factor, jnp.sin(angle) * factor)


def complex_table(row_count, col_count, length, direction, factor):
    cosine, sine = phase_pair(row_count, col_count, length, direction, factor)
    upper = jnp.stack([cosine, -sine], axis=1)
    lower = jnp.stack([sine, cosine], axis=1)
    return jnp.stack([upper, lower]).astype(jnp.bfloat16)


def apply_table(table, data, part_dim, index_dim):
    return lax.dot_general(
        table, data, (((2, 3), (part_dim, index_dim)), ((), ())), preferred_element_type=jnp.float32
    )


def compress(echoes, range_phase):
    cosine = jnp.cos(range_phase)
    sine = jnp.sin(range_phase)
    real_in = echoes[0].astype(jnp.float32)
    imag_in = echoes[1].astype(jnp.float32)
    spectrum = jnp.stack(
        [real_in * cosine - imag_in * sine, real_in * sine + imag_in * cosine]
    ).astype(jnp.bfloat16)
    channels = spectrum.shape[1]
    pulses = spectrum.shape[2]
    range_bins = spectrum.shape[3]
    second = range_bins // R1
    spectrum = spectrum.reshape((2, channels, pulses, R1, second))
    section = apply_table(complex_table(R1, R1, R1, 1.0, 1.0), spectrum, 0, 3)
    twist_re, twist_im = phase_pair(R1, second, range_bins, 1.0, 1.0 / math.sqrt(range_bins))
    twist_re = twist_re[:, None, None, :]
    twist_im = twist_im[:, None, None, :]
    partial_terms = jnp.stack(
        [
            section[0] * twist_re - section[1] * twist_im,
            section[0] * twist_im + section[1] * twist_re,
        ]
    ).astype(jnp.bfloat16)
    result = apply_table(
        complex_table(second, second, second, 1.0, 1.0), partial_terms, 0, 4
    ).astype(jnp.bfloat16)
    return result.transpose(0, 3, 4, 1, 2).reshape((2, channels, pulses, range_bins))


def doppler(window):
    wide = window.shape[2]
    forward = complex_table(wide, wide, wide, -1.0, 1.0 / math.sqrt(wide))
    return apply_table(forward, window, 0, 2).astype(jnp.bfloat16)


def migrate(extended, offsets, tap_weights, block):
    tile = min(128, block)
    taps = tap_weights.shape[0]
    pieces = []
    for tile_index in range(block // tile):
        first = tile_index * tile
        rows_here = jnp.arange(tile, dtype=jnp.int32)
        target = rows_here + offsets[first : first + tile]
        columns = jnp.arange(tile + MARG, dtype=jnp.int32)
        tap_range = jnp.arange(taps, dtype=jnp.int32)
        onehot = (
            columns[None, None, :] == target[None, :, None] + tap_range[:, None, None]
        ).astype(jnp.bfloat16)
        window_part = extended[:, :, :, first : first + tile + MARG]
        picked = lax.dot_general(
            window_part, onehot, (((3,), (2,)), ((), ())), preferred_element_type=jnp.float32
        )
        total = jnp.zeros(picked.shape[:3] + (tile,), jnp.float32)
        for tap_index in range(taps):
            total = total + picked[:, :, :, tap_index] * tap_weights[tap_index][None, :, None, None]
        pieces.append(total)
    return jnp.concatenate(pieces, axis=3)


def body(echoes, range_phase, offsets, tap_weights, channel_mix, azimuth_filter):
    dev_count = lax.axis_size("dev")
    compressed = compress(echoes, range_phase)
    range_bins = compressed.shape[3]
    block = range_bins // dev_count
    turned = lax.all_to_all(compressed, "dev", split_axis=3, concat_axis=2, tiled=True)
    group_pulses = turned.shape[2]
    intersection = group_pulses // 2
    following = shifted(turned[:, :, :intersection], "blk", -1)
    spectra = doppler(jnp.concatenate([turned, following], axis=2))
    border = shifted(spectra[:, :, :, :MARG], "dev", -1)
    extended = jnp.concatenate([spectra, border], axis=3)
    wide = extended.shape[1]
    channels = extended.shape[2]
    moved = migrate(extended, offsets, tap_weights, block)
    mix_real = (
        azimuth_filter[0][:, None, :] * channel_mix[0]
        - azimuth_filter[1][:, None, :] * channel_mix[1]
    )
    mix_imag = (
        azimuth_filter[0][:, None, :] * channel_mix[1]
        + azimuth_filter[1][:, None, :] * channel_mix[0]
    )
    rows_real = []
    rows_imag = []
    for channel in range(channels):
        sum_real = jnp.zeros((wide, block), jnp.float32)
        sum_imag = jnp.zeros((wide, block), jnp.float32)
        for other_chan in range(channels):
            coef_real = mix_real[channel, other_chan][:, None]
            coef_imag = mix_imag[channel, other_chan][:, None]
            sum_real = (
                sum_real + coef_real * moved[0, :, other_chan] - coef_imag * moved[1, :, other_chan]
            )
            sum_imag = (
                sum_imag + coef_real * moved[1, :, other_chan] + coef_imag * moved[0, :, other_chan]
            )
        rows_real.append(sum_real)
        rows_imag.append(sum_imag)
    focused = jnp.stack([jnp.stack(rows_real, axis=1), jnp.stack(rows_imag, axis=1)]).astype(
        jnp.bfloat16
    )
    backward = complex_table(group_pulses, wide, wide, 1.0, 1.0 / math.sqrt(wide))
    image = apply_table(backward, focused, 0, 1).astype(jnp.bfloat16)
    return image.transpose(0, 2, 1, 3)


def solution(mesh):
    in_specs = (P(None, None, ("blk", "dev"), None), P(), P("dev"), P(), P(), P())
    out_specs = P(None, None, "blk", "dev")
    return jax.shard_map(body, mesh=mesh, in_specs=in_specs, out_specs=out_specs, check_vma=False)
```

profile of v0, /device:TPU:0, one launch (start us, length us, event | category | flops | bytes accessed | tf_op | source)
XLA Modules:
  0.0 256.4 jit_solution(17232224842933385745)
XLA Ops:
  0.8 1.1 fusion.138
  1.9 2.2 fusion.88
  4.1 0.6 copy_bitcast_fusion
  4.7 0.7 convolution_bitcast_fusion
  5.5 0.6 subtract_convert_fusion
  6.1 0.7 fusion.15
  6.8 24.4 %copy.105 = bf16[2,4,8,128,128]{2,1,0,4,3:T(4,128)(2,1)} copy(bf16[2,4,8,128,128]{4,3,2,1,0:T(8,128)(2,1)S(1)} %fusion.15) | data formatting | bytes 4194304 | tf_op jit(solution)/shard_map/reshape | solution.py:67
  31.2 39.5 %reshape.3041 = bf16[32,2,16384]{2,1,0:T(2,128)(2,1)} reshape(bf16[16384,2,4,8]{3,2,1,0:T(4,128)(2,1)} %bitcast.547) | data formatting | bytes 4194304
  70.8 7.3 %all-to-all-start = ((bf16[32,2,16384]{2,1,0:T(2,128)(2,1)}), bf16[32,2,16384]{2,1,0:T(2,128)(2,1)S(1)}, u32[]{:S(2)}, u32[]{:S(2)}) async-start(bf16[32,2,16384]{2,1,0:T(2,128)(2,1)} %reshape.3041), calls=%async_computation | async-start | bytes 4194304 | tf_op jit(solution)/shard_map/all_to_all | solution.py:105
  78.1 0.7 slice_reduce_fusion.30
  78.8 0.7 slice_reduce_fusion.31
  79.5 1.5 fusion.116
  81.0 2.3 fusion.106
  83.4 1.7 negate_convert_fusion.1
  85.1 2.6 %negate_convert_fusion = (bf16[384,1,384]{2,0,1:T(8,128)(2,1)S(1)}, bf16[384,1,384]{2,0,1:T(8,128)(2,1)S(1)}) fusion(), kind=kLoop, calls=%fused_computation.176 | loop fusion | flops 2064384 | bytes 589824 | tf_op jit(solution)/shard_map/convert.33
  87.7 0.8 maximum_bitcast_fusion.16
  88.5 38.4 %all-to-all-done = bf16[32,2,16384]{2,1,0:T(2,128)(2,1)S(1)} async-done(((bf16[32,2,16384]{2,1,0:T(2,128)(2,1)}), bf16[32,2,16384]{2,1,0:T(2,128)(2,1)S(1)}, u32[]{:S(2)}, u32[]{:S(2)}) %all-to-all-start) | async-done | bytes 2097184 | tf_op jit(solution)/shard_map/all_to_all | solution.py:105
  127.0 40.6 %reshape.3042 = bf16[16384,2,4,8]{3,2,1,0:T(4,128)(2,1)} reshape(bf16[32,2,16384]{2,1,0:T(2,128)(2,1)S(1)} %all-to-all-done) | data formatting | bytes 4194304
  167.6 40.2 %copy.47 = bf16[2,4,8,32,512]{4,2,3,0,1:T(8,128)(2,1)S(1)} copy(bf16[2,4,8,32,512]{2,1,0,4,3:T(4,128)(2,1)} %bitcast.548) | data formatting | bytes 4194304 | tf_op jit(solution)/shard_map/all_to_all | solution.py:105
  207.9 0.9 collective-permute-start
  208.8 0.6 slice_reduce_fusion.39
  209.7 0.6 iota_add_fusion.3
  210.3 4.4 %bitcast_convert_fusion = bf16[2,384,4,512]{3,1,2,0:T(8,128)(2,1)S(1)} fusion(bf16[2,4,128,512]{3,2,0,1:T(8,128)(2,1)S(1)} %collective-permute-done, bf16[2,4,256,512]{3,2,0,1:T(8,128)(2,1)} %bitcast.550, bf16[1,384,2,384]{3,1,2,0:T(8,128)(2,1)S(1)} %get-tuple-element.50, bf16[1,384,2,384]{3,1,2,0:T(8,128)(2,1)S(1)} %get-tuple-element.49), kind=kOutput, calls=%fused_computation.1 | convolution fusion | flops 2426142720 | bytes 7471104 | tf_op jit(solution)/shard_map/dot_general | solution.py:36
  214.7 1.0 slice.509
  215.7 2.1 copy.74
  217.9 1.3 collective-permute-start.1
  219.2 1.8 fusion.52
  221.0 1.8 fusion.68
  222.9 6.4 %fusion.84 = f32[2,384,4,8,128]{1,4,3,2,0:T(8,128)} fusion(bf16[2,384,4,512]{3,1,2,0:T(8,128)(2,1)S(1)} %bitcast_convert_fusion, s32[8,128]{1,0:T(8,128)S(1)} %copy-done.51), kind=kOutput, calls=%fused_computation.132 | convolution fusion | flops 1208156160 | bytes 14159872 | tf_op jit(solution)/shard_map/dot_general | solution.py:90
  229.4 2.3 fusion.38
  231.7 2.3 fusion.54
  234.0 2.8 %copy-done = f32[2,384,4,8,128]{1,4,3,2,0:T(8,128)S(1)} copy-done((f32[2,384,4,8,128]{1,4,3,2,0:T(8,128)S(1)}, f32[2,384,4,8,128]{1,4,3,2,0:T(8,128)}, u32[]{:S(2)}) %copy-start) | copy-done | bytes 12582936
  236.8 2.3 fusion.70
  239.1 2.2 copy.75
  241.3 3.0 %fusion.34 = f32[2,384,4,8,128]{1,4,2,0,3:T(8,128)S(1)} fusion(bf16[2,384,4,64]{3,1,2,0:T(8,128)(2,1)} %copy.75, bf16[2,384,4,512]{3,1,2,0:T(8,128)(2,1)S(1)} %bitcast_convert_fusion, s32[8,128]{1,0:T(8,128)S(1)} %iota_add_fusion), kind=kOutput, calls=%fused_computation.56 | convolution fusion | flops 1210515456 | bytes 16125952 | tf_op jit(solution)/shard_map/dot_general | solution.py:90
  244.4 1.1 fusion.19
  245.7 0.5 copy-done.2
  246.2 0.5 copy-done.3
  246.7 0.7 pad_maximum_fusion
  247.5 0.4 subtract_convert_fusion.3
  248.0 0.4 add_convert_fusion.3
  248.7 0.4 subtract_convert_fusion.4
  249.2 0.4 add_convert_fusion.4
  249.9 0.4 subtract_convert_fusion.2
  250.4 0.4 add_convert_fusion.2
  251.1 0.4 subtract_convert_fusion.1
  252.5 0.7 copy-done.5
  253.2 3.1 %fusion.10 = bf16[2,4,256,512]{3,2,1,0:T(8,128)(2,1)} fusion(bf16[1,384,4,512]{1,3,2,0:T(8,128)(2,1)S(1)} %maximum_bitcast_fusion.11, bf16[1,384,4,512]{1,3,2,0:T(8,128)(2,1)S(1)} %maximum_bitcast_fusion.10, bf16[1,256,2,384]{3,1,2,0:T(8,128)(2,1)S(1)} %copy-done.5, bf16[1,256,2,384]{3,1,2,0:T(8,128)(2,1)S(1)} %get-tuple-element.51), kind=kOutput, calls=%fused_computation.21 | convolution fusion | flops 1619525632 | bytes 6029312 | tf_op jit(solution)/shard_map/dot_general | solution.py:36
  (122 shorter events, 3.1 us)
Async XLA Ops:
  70.8 7.3 %copy-start.53 = (f32[2,4,384]{2,1,0:T(4,128)S(1)}, f32[2,4,384]{2,1,0:T(4,128)}, u32[]{:S(2)}) copy-start(f32[2,4,384]{2,1,0:T(4,128)} %param.11) | copy-start | bytes 36868
  70.8 7.3 %copy-start.18 = (f32[2,4,4,384]{3,2,1,0:T(4,128)S(1)}, f32[2,4,4,384]{3,2,1,0:T(4,128)}, u32[]{:S(2)}) copy-start(f32[2,4,4,384]{3,2,1,0:T(4,128)} %param.10) | copy-start | bytes 147460
  70.8 56.2 %all-to-all-start = ((bf16[32,2,16384]{2,1,0:T(2,128)(2,1)}), bf16[32,2,16384]{2,1,0:T(2,128)(2,1)S(1)}, u32[]{:S(2)}, u32[]{:S(2)}) async-start(bf16[32,2,16384]{2,1,0:T(2,128)(2,1)} %reshape.3041), calls=%async_computation | async-start | bytes 4194304 | tf_op jit(solution)/shard_map/all_to_all | solution.py:105
  207.8 1.8 copy-start.4
  207.8 1.0 copy-start.52
  207.8 1.8 copy-start.54
  207.9 2.4 collective-permute-start
  217.9 21.2 %collective-permute-start.1 = (bf16[2,384,4,64]{1,3,2,0:T(8,128)(2,1)}, bf16[2,384,4,64]{1,3,2,0:T(8,128)(2,1)}, u32[]{:S(2)}, u32[]{:S(2)}) collective-permute-start(bf16[2,384,4,64]{1,3,2,0:T(8,128)(2,1)} %copy.74), channel_id=1, source_target_pairs={{1,0},{2,1},{3,2},{4,3},{5,4},{6,5},{7,6},{8,7},{9,8},{10,9},{11,1... | collective-permute-start | bytes 1179656 | tf_op jit(solution)/shard_map/ppermute | solution.py:15
  221.0 1.9 copy-start.51
  222.9 6.5 %copy-start.6 = (f32[384]{0:T(512)S(1)}, f32[384]{0:T(512)}, u32[]{:S(2)}) copy-start(f32[384]{0:T(512)} %get-tuple-element.38) | copy-start | bytes 4612
  222.9 6.5 %copy-start.7 = (f32[384]{0:T(512)S(1)}, f32[384]{0:T(512)}, u32[]{:S(2)}) copy-start(f32[384]{0:T(512)} %get-tuple-element.39) | copy-start | bytes 4612
  222.9 6.5 %copy-start.8 = (f32[384]{0:T(512)S(1)}, f32[384]{0:T(512)}, u32[]{:S(2)}) copy-start(f32[384]{0:T(512)} %get-tuple-element.40) | copy-start | bytes 4612
  222.9 6.5 %copy-start.10 = (f32[384]{0:T(512)S(1)}, f32[384]{0:T(512)}, u32[]{:S(2)}) copy-start(f32[384]{0:T(512)} %get-tuple-element.41) | copy-start | bytes 4612
  222.9 6.5 %copy-start.12 = (f32[384]{0:T(512)S(1)}, f32[384]{0:T(512)}, u32[]{:S(2)}) copy-start(f32[384]{0:T(512)} %get-tuple-element.42) | copy-start | bytes 4612
  222.9 6.5 %copy-start.14 = (f32[384]{0:T(512)S(1)}, f32[384]{0:T(512)}, u32[]{:S(2)}) copy-start(f32[384]{0:T(512)} %get-tuple-element.43) | copy-start | bytes 4612
  222.9 6.5 %copy-start.16 = (f32[384]{0:T(512)S(1)}, f32[384]{0:T(512)}, u32[]{:S(2)}) copy-start(f32[384]{0:T(512)} %get-tuple-element.44) | copy-start | bytes 4612
  231.7 5.1 %copy-start = (f32[2,384,4,8,128]{1,4,3,2,0:T(8,128)S(1)}, f32[2,384,4,8,128]{1,4,3,2,0:T(8,128)}, u32[]{:S(2)}) copy-start(f32[2,384,4,8,128]{1,4,3,2,0:T(8,128)} %fusion.84) | copy-start | bytes 37748740
  241.3 3.0 %copy-start.9 = (f32[384]{0:T(512)S(1)}, f32[384]{0:T(512)}, u32[]{:S(2)}) copy-start(f32[384]{0:T(512)} %get-tuple-element.40) | copy-start | bytes 4612
  241.3 3.0 %copy-start.11 = (f32[384]{0:T(512)S(1)}, f32[384]{0:T(512)}, u32[]{:S(2)}) copy-start(f32[384]{0:T(512)} %get-tuple-element.41) | copy-start | bytes 4612
  241.3 3.0 %copy-start.13 = (f32[384]{0:T(512)S(1)}, f32[384]{0:T(512)}, u32[]{:S(2)}) copy-start(f32[384]{0:T(512)} %get-tuple-element.42) | copy-start | bytes 4612
  241.3 3.0 %copy-start.15 = (f32[384]{0:T(512)S(1)}, f32[384]{0:T(512)}, u32[]{:S(2)}) copy-start(f32[384]{0:T(512)} %get-tuple-element.43) | copy-start | bytes 4612
  241.3 3.0 %copy-start.17 = (f32[384]{0:T(512)S(1)}, f32[384]{0:T(512)}, u32[]{:S(2)}) copy-start(f32[384]{0:T(512)} %get-tuple-element.44) | copy-start | bytes 4612
  244.3 1.4 copy-start.1
  244.3 1.9 copy-start.2
  244.4 2.3 copy-start.3
  246.7 0.7 copy-start.35
  246.7 0.7 copy-start.36
  246.7 0.8 copy-start.37
  246.7 0.8 copy-start.38
  246.7 0.8 copy-start.47
  246.7 0.8 copy-start.48
  246.7 0.8 copy-start.49
  246.7 0.8 copy-start.50
  248.0 0.7 copy-start.27
  248.0 0.7 copy-start.29
  248.0 0.7 copy-start.30
  248.0 0.7 copy-start.43
  248.0 0.7 copy-start.44
  248.0 0.7 copy-start.45
  248.0 0.7 copy-start.46
  249.2 0.7 copy-start.23
  249.2 0.7 copy-start.24
  249.2 0.7 copy-start.39
  249.2 0.7 copy-start.41
  250.3 0.7 copy-start.19
  250.3 0.7 copy-start.20
  250.4 0.7 copy-start.34
  252.2 1.0 copy-start.5
  (10 other events, 6.7 us)
where the time goes:
time: 259 us; the launch traced here: 256 us
  local copies, waits for them, and re-layouts  159 us (61%)
  waiting for transfers between devices  38.4 us (15%)
  other arithmetic  26.1 us (10%)
  matrix products  22.1 us (9%)
  starting transfers between devices  9.48 us (4%)
    unnamed x112, local copies, waits for them, and re-layouts  85.8 us
    all_to_all x1, local copies, waits for them, and re-layouts, body(): lax.all_to_all(compressed, 'dev', split_axis=3, concat_axis=2, tiled=True)  40.2 us
    all_to_all x1, waiting for transfers between devices, body(): lax.all_to_all(compressed, 'dev', split_axis=3, concat_axis=2, tiled=True)  38.4 us
    reshape x1, local copies, waits for them, and re-layouts, compress(): result.transpose(0, 3, 4, 1, 2).reshape((2, channels, pulses, range_bins))  24.4 us
    dot_general x4, matrix products, migrate(): lax.dot_general(window_part, onehot, (((3,), (2,)), ((), ())), preferred_...  13.1 us
    another operation x15, other arithmetic  12.8 us
    dot_general x4, matrix products, apply_table(): lax.dot_general(table, data, (((2, 3), (part_dim, index_dim)), ((), ())),...  9.03 us
    add x4, other arithmetic, migrate(): total + picked[:, :, :, tap_index] * tap_weights[tap_index][None, :, None...  8 us
  transfers between devices with their start and end apart: 3, of which 1 were waited for; matrix products, arithmetic and copies ran while one was open for 11% of the time, Pallas kernels for 0%

commit v1 on v0

v1 whole, which is shorter than its diff:
```python
import functools
import math

import jax
import jax.numpy as jnp
import numpy as np
from jax import lax
from jax.experimental import pallas as pl
from jax.experimental.pallas import tpu as pltpu
from jax.sharding import PartitionSpec as P

R1 = 128
LANES = 128
MARG = 64
F32 = jnp.float32
BF16 = jnp.bfloat16
MESH = pl.DeviceIdType.MESH


def phases(rows, cols, length):
    product = np.outer(rows, cols) % length
    angle = product.astype(np.float64) * (2.0 * math.pi / length)
    return np.cos(angle), np.sin(angle)


def range_table():
    index = np.arange(R1)
    cosine, sine = phases(index, index, R1)
    return np.block([[cosine, -sine], [sine, cosine]]).astype(BF16)


def twist_tables(range_bins):
    cosine, sine = phases(np.arange(R1), np.arange(range_bins // R1), range_bins)
    scale = 1.0 / math.sqrt(range_bins)
    return np.stack([cosine * scale, sine * scale]).astype(np.float32)


def doppler_table(pulse_of_row, wide):
    senders, pulses = pulse_of_row.shape
    cosine, sine = phases(pulse_of_row.reshape(-1), np.arange(wide), wide)
    keep = (pulse_of_row.reshape(-1) >= 0)[:, None] / math.sqrt(wide)
    real = (cosine * keep).reshape(senders, 1, pulses, wide)
    imag = (-sine * keep).reshape(senders, 1, pulses, wide)
    from_real = np.concatenate([real, imag], axis=3)
    from_imag = np.concatenate([-imag, real], axis=3)
    return np.concatenate([from_real, from_imag], axis=1).reshape(-1, 2 * wide).astype(BF16)


def image_table(pulses, wide):
    cosine, sine = phases(np.arange(pulses), np.arange(wide), wide)
    scale = 1.0 / math.sqrt(wide)
    return (np.block([[cosine, -sine], [sine, cosine]]) * scale).astype(BF16)


def cos_sin(angle):
    y = angle * 0.25
    z = y * y
    sine = y * (1 + z * (-1 / 6 + z * (1 / 120 + z * (-1 / 5040 + z * (1 / 362880 - z / 39916800)))))
    vers = z * (0.5 + z * (-1 / 24 + z * (1 / 720 + z * (-1 / 40320 + z / 3628800))))
    for _ in range(2):
        sine, vers = 2 * sine * (1 - vers), 2 * sine * sine
    return 1 - vers, sine


def kernel(
    n, pulses, wide, tiles,
    echo_ref, phase_ref, offs_ref, taps_ref, mix_ref, filt_ref,
    rng_ref, twist_ref, fwd_ref, back_ref,
    out_ref,
    raw, spec, part, comp, send, recv, halo, dop, foc, img, phase, coef,
    send_sem, first_sem, tile_sem, halo_send, halo_recv,
):
    me = lax.axis_index("dev")
    channels = echo_ref.shape[1]
    taps = taps_ref.shape[0]
    rows = 2 * pulses
    block = tiles * LANES
    group_pulses = out_ref.shape[2]

    barrier = pltpu.get_barrier_semaphore()

    @pl.loop(1, n)
    def _(i):
        pl.semaphore_signal(
            barrier, inc=1, device_id={"dev": lax.rem(me + i, n)}, device_id_type=MESH
        )

    cosine, sine = cos_sin(phase_ref[...])
    phase[0] = cosine
    phase[1] = sine

    def range_channel(c):
        for ri in range(2):
            for k in range(R1):
                raw[ri, k * pulses : (k + 1) * pulses, :] = echo_ref[
                    ri, c, :, k * LANES : (k + 1) * LANES
                ].astype(F32)
        for q in range(pulses):
            real = raw[0, pl.ds(q, R1, stride=pulses), :]
            imag = raw[1, pl.ds(q, R1, stride=pulses), :]
            cosine = phase[0]
            sine = phase[1]
            at = slice(q * LANES, (q + 1) * LANES)
            spec[:R1, at] = (real * cosine - imag * sine).astype(BF16)
            spec[R1:, at] = (real * sine + imag * cosine).astype(BF16)
        half = 4
        for q0 in range(0, pulses, half):
            span = slice(q0 * LANES, (q0 + half) * LANES)
            section = jnp.dot(rng_ref[...], spec[:, span], preferred_element_type=F32)
            for q in range(half):
                real = section[:R1, q * LANES : (q + 1) * LANES]
                imag = section[R1:, q * LANES : (q + 1) * LANES]
                at = slice((q0 + q) * LANES, (q0 + q + 1) * LANES)
                part[at, :LANES] = (real * twist_ref[0] - imag * twist_ref[1]).astype(BF16)
                part[at, LANES:] = (real * twist_ref[1] + imag * twist_ref[0]).astype(BF16)
            result = lax.dot_general(
                rng_ref[...], part[span, :], (((1,), (1,)), ((), ())), preferred_element_type=F32
            )
            for q in range(half):
                at = slice(q * LANES, (q + 1) * LANES)
                comp[pl.ds(q0 + q, R1, stride=rows), :] = result[:R1, at]
                comp[pl.ds(pulses + q0 + q, R1, stride=rows), :] = result[R1:, at]
        for first in range(0, R1, 16):
            piece = comp[first * rows : (first + 16) * rows, :]
            send[c, first : first + 16] = piece.reshape(16, rows, LANES).astype(BF16)

    def first_copy(c, peer):
        return pltpu.make_async_remote_copy(
            src_ref=send.at[c, peer * tiles],
            dst_ref=recv.at[0, c, me],
            send_sem=send_sem,
            recv_sem=first_sem,
            device_id={"dev": peer},
            device_id_type=MESH,
        )

    def tile_copy(t, peer):
        return pltpu.make_async_remote_copy(
            src_ref=send.at[:, peer * tiles + t],
            dst_ref=recv.at[t, :, me],
            send_sem=send_sem,
            recv_sem=tile_sem.at[t],
            device_id={"dev": peer},
            device_id_type=MESH,
        )

    @pl.loop(0, channels)
    def _(c):
        range_channel(c)

        @pl.when(c == 0)
        def _():
            pl.semaphore_wait(barrier, n - 1)

        @pl.loop(1, n)
        def _(i):
            first_copy(c, lax.rem(me + i, n)).start()

        recv[0, c, me] = send[c, me * tiles]

    @pl.loop(1, tiles)
    def _(i):
        t = tiles - i

        @pl.loop(1, n)
        def _(j):
            tile_copy(t, lax.rem(me + j, n)).start()

        for c in range(channels):
            recv[t, c, me] = send[c, me * tiles + t]

    for c in range(channels):
        for ri in range(2):
            other = mix_ref[1 - ri, c]
            sign = -1.0 if ri == 0 else 1.0
            coef[ri, c] = (
                filt_ref[0, c : c + 1, :] * mix_ref[ri, c]
                + sign * filt_ref[1, c : c + 1, :] * other
            )

    def spectra(load, first, count):
        window = jnp.concatenate(
            [load(c).reshape(n * rows, LANES)[:, :count] for c in range(channels)], axis=1
        )
        result = lax.dot_general(
            window, fwd_ref[...], (((0,), (0,)), ((), ())), preferred_element_type=F32
        ).astype(BF16).astype(F32)
        for c in range(channels):
            dop[c, pl.ds(first, count), :] = result[c * count : (c + 1) * count]

    def focus_rows(first, start, stop):
        @pl.loop(start, stop)
        def _(step):
            row = pl.multiple_of(step * 16, 16)
            base = pl.multiple_of(first + row, 16)
            near = dop.at[:, pl.ds(base, 24), :]
            for f in range(wide // LANES):
                at = slice(f * LANES, (f + 1) * LANES)
                moved = []
                for d in range(channels):
                    pair = []
                    for ri in range(2):
                        where = slice(ri * wide + f * LANES, ri * wide + (f + 1) * LANES)
                        total = near[d, :16, where] * taps_ref[0:1, at]
                        for j in range(1, taps):
                            total = total + near[d, j : j + 16, where] * taps_ref[j : j + 1, at]
                        pair.append(total)
                    moved.append(pair)
                for c in range(channels):
                    real = imag = None
                    for d in range(channels):
                        re, im = moved[d]
                        cre = coef[0, c, d : d + 1, at]
                        cim = coef[1, c, d : d + 1, at]
                        new_real = cre * re - cim * im
                        new_imag = cre * im + cim * re
                        real = new_real if d == 0 else real + new_real
                        imag = new_imag if d == 0 else imag + new_imag
                    foc[c, pl.ds(row, 16), at] = real.astype(BF16)
                    foc[c, pl.ds(row, 16), wide + f * LANES : wide + (f + 1) * LANES] = imag.astype(BF16)

    def image(slot, count):
        columns = foc[:, :count, :].reshape(channels * count, 2 * wide)
        result = lax.dot_general(
            back_ref[...], columns, (((1,), (1,)), ((), ())), preferred_element_type=F32
        ).astype(BF16)
        for c in range(channels):
            img[slot, c, :, :count] = result[:, c * count : (c + 1) * count]

    def pick(t):
        target = offs_ref[pl.ds(t, 1), :] + lax.broadcasted_iota(jnp.int32, (1, LANES), 1)
        source = lax.broadcasted_iota(jnp.int32, (2 * LANES, LANES), 0)
        onehot = jnp.where(source == target, 1.0, 0.0).astype(BF16)
        for c in range(channels):
            both = jnp.concatenate([img[t, c], img[t + 1, c]], axis=1)
            result = jnp.dot(both, onehot, preferred_element_type=F32).astype(BF16)
            for ri in range(2):
                out_ref[ri, c, :, pl.ds(pl.multiple_of(t * LANES, LANES), LANES)] = result[
                    ri * group_pulses : (ri + 1) * group_pulses
                ]

    def wait_bytes(sem, ref):
        pltpu.make_async_copy(ref, ref, sem).wait()

    wait_bytes(first_sem, recv.at[0, :, : n - 1])
    dop[:, block + MARG :, :] = jnp.zeros_like(dop[:, block + MARG :, :])
    img[tiles, :, :, MARG:] = jnp.zeros_like(img[tiles, :, :, MARG:])

    halo_copy = pltpu.make_async_remote_copy(
        src_ref=recv.at[0],
        dst_ref=halo,
        send_sem=halo_send,
        recv_sem=halo_recv,
        device_id={"dev": lax.rem(me + n - 1, n)},
        device_id_type=MESH,
    )

    @pl.when(me > 0)
    def _():
        halo_copy.start()

    spectra(lambda c: recv[0, c], 0, LANES)

    @pl.when(me < n - 1)
    def _():
        halo_copy.wait_recv()

    @pl.when(me == n - 1)
    def _():
        halo[...] = jnp.zeros_like(halo)

    spectra(lambda c: halo[c], block, MARG)
    focus_rows(block, 0, MARG // 16)
    image(tiles, MARG)

    @pl.loop(1, tiles)
    def _(i):
        t = tiles - i
        wait_bytes(tile_sem.at[t], recv.at[t, :, : n - 1])
        first = pl.multiple_of(t * LANES, LANES)
        spectra(lambda c: recv[t, c], first, LANES)
        focus_rows(first, 0, LANES // 16)
        image(t, LANES)
        pick(t)

    focus_rows(0, 0, LANES // 16)
    image(0, LANES)
    pick(0)

    wait_bytes(send_sem, send.at[:, : (n - 1) * tiles])

    @pl.when(me > 0)
    def _():
        halo_copy.wait_send()


def body(echoes, range_phase, offsets, tap_weights, channel_mix, azimuth_filter):
    n = lax.axis_size("dev")
    groups = lax.axis_size("blk")
    channels, own, range_bins = echoes.shape[1:]
    block = range_bins // n
    tiles = block // LANES
    wide = tap_weights.shape[1]
    group_pulses = own * n
    pulse_of_row = np.arange(group_pulses).reshape(n, own)
    if groups > 1:
        following = lax.ppermute(echoes, "blk", [(i, i - 1) for i in range(1, groups)])
        echoes = jnp.concatenate([echoes, following], axis=2)
        later = pulse_of_row + group_pulses
        later = np.where(later < wide, later, -1)
        pulse_of_row = np.concatenate([pulse_of_row, later], axis=1)
    pulses = echoes.shape[2]
    rows = 2 * pulses
    vmem = pl.BlockSpec(memory_space=pltpu.VMEM)
    call = pl.pallas_call(
        functools.partial(kernel, n, pulses, wide, tiles),
        out_shape=jax.ShapeDtypeStruct((2, channels, group_pulses, block), BF16),
        in_specs=[vmem] * 10,
        out_specs=vmem,
        scratch_shapes=[
            pltpu.VMEM((2, R1 * pulses, LANES), F32),
            pltpu.VMEM((2 * R1, pulses * LANES), BF16),
            pltpu.VMEM((pulses * LANES, 2 * LANES), BF16),
            pltpu.VMEM((R1 * rows, LANES), F32),
            pltpu.VMEM((channels, R1, rows, LANES), BF16),
            pltpu.VMEM((tiles, channels, n, rows, LANES), BF16),
            pltpu.VMEM((channels, n, rows, LANES), BF16),
            pltpu.VMEM((channels, block + MARG + 16, 2 * wide), F32),
            pltpu.VMEM((channels, LANES, 2 * wide), BF16),
            pltpu.VMEM((tiles + 1, channels, 2 * group_pulses, LANES), BF16),
            pltpu.VMEM((2, R1, LANES), F32),
            pltpu.VMEM((2, channels, channels, wide), F32),
            pltpu.SemaphoreType.DMA,
            pltpu.SemaphoreType.DMA,
            pltpu.SemaphoreType.DMA((tiles,)),
            pltpu.SemaphoreType.DMA,
            pltpu.SemaphoreType.DMA,
        ],
        compiler_params=pltpu.CompilerParams(
            collective_id=0, has_side_effects=True, vmem_limit_bytes=56 * 1024 * 1024
        ),
        cost_estimate=pl.CostEstimate(
            flops=6 * 10**9, bytes_accessed=8 * 2**20, transcendentals=0
        ),
        name="focus",
    )
    return call(
        echoes,
        range_phase.reshape(R1, range_bins // R1),
        offsets.reshape(tiles, LANES),
        tap_weights,
        channel_mix,
        azimuth_filter,
        jnp.asarray(range_table()),
        jnp.asarray(twist_tables(range_bins)),
        jnp.asarray(doppler_table(pulse_of_row, wide)),
        jnp.asarray(image_table(group_pulses, wide)),
    )


def solution(mesh):
    in_specs = (P(None, None, ("blk", "dev"), None), P(), P("dev"), P(), P(), P())
    out_specs = P(None, None, "blk", "dev")
    return jax.shard_map(body, mesh=mesh, in_specs=in_specs, out_specs=out_specs, check_vma=False)
```

time: 259 us -> 84.3 us (0.33)
  the two profiles are of different devices: /device:TPU:0 before, /device:TPU:15 now
where the time goes in v1:
time: 84.3 us; the launch traced here: 84.2 us
  Pallas kernels  81.1 us (96%)
  local copies, waits for them, and re-layouts  3.05 us (4%)
    pallas_call x1, Pallas kernels, body(): call(echoes, range_phase.reshape(R1, range_bins // R1), offsets.reshape(t...  81.1 us
    unnamed x1, local copies, waits for them, and re-layouts  3.05 us

profile of v1, /device:TPU:15, one launch (start us, length us, event | category | flops | bytes accessed | tf_op | source)
XLA Modules:
  0.0 84.2 jit_solution(8388283927506654111)
XLA Ops:
  0.0 81.1 %focus.1 = bf16[2,4,256,512]{3,2,1,0:T(8,128)(2,1)} custom-call(bf16[2,4,8,16384]{3,2,1,0:T(8,128)(2,1)} %echo_ref.1, f32[128,128]{1,0:T(8,128)} %bitcast.2, s32[4,128]{1,0:T(4,128)} %bitcast.3, f32[8,384]{1,0:T(8,128)} %taps_ref.1, f32[2,4,4,384]{3,2,1,0:T(4,128)} %mix_ref.1, f32[2,4,384]{2,1,0:T(4,128)} %filt_ref.1, ...), custom_call_target="tpu_custom_call" | custom-call | flops 6000000000 | bytes 8388608 | tf_op jit(solution)/shard_map/focus/pallas_call | solution.py:347
  81.2 3.0 %copy.12 = bf16[2,4,256,512]{3,2,1,0:T(8,128)(2,1)} copy(bf16[2,4,256,512]{3,2,1,0:T(8,128)(2,1)} %focus.1) | data formatting | bytes 4194304

commit v2 on v1

--- a/solution.py
+++ b/solution.py
@@ -12,6 +12,7 @@
 R1 = 128
 LANES = 128
 MARG = 64
+PLANE = 8
 F32 = jnp.float32
 BF16 = jnp.bfloat16
 MESH = pl.DeviceIdType.MESH
@@ -63,12 +64,12 @@
 
 
 def kernel(
-    n, pulses, wide, tiles,
+    n, pulses, wide, tiles, edges,
     echo_ref, phase_ref, offs_ref, taps_ref, mix_ref, filt_ref,
     rng_ref, twist_ref, fwd_ref, back_ref,
     out_ref,
-    raw, spec, part, comp, send, recv, halo, dop, foc, img, phase, coef,
-    send_sem, first_sem, tile_sem, halo_send, halo_recv,
+    raw, spec, part, comp, send, recv, halo, dop, foc, early, img, phase, coef,
+    send_sem, first_sem, tile_sem, halo_send, halo_recv, edge_send,
 ):
     me = lax.axis_index("dev")
     channels = echo_ref.shape[1]
@@ -76,6 +77,11 @@
     rows = 2 * pulses
     block = tiles * LANES
     group_pulses = out_ref.shape[2]
+
+    stride = next(s for s in (11, 7, 5, 3, 1) if math.gcd(s, n) == 1)
+
+    def peer_of(i):
+        return lax.rem(me + stride * i, n)
 
     barrier = pltpu.get_barrier_semaphore()
 
@@ -154,9 +160,29 @@
 
         @pl.loop(1, n)
         def _(i):
-            first_copy(c, lax.rem(me + i, n)).start()
+            first_copy(c, peer_of(i)).start()
 
         recv[0, c, me] = send[c, me * tiles]
+
+    def edge_copy(b):
+        return pltpu.make_async_remote_copy(
+            src_ref=send.at[:, b * tiles],
+            dst_ref=halo.at[:, me],
+            send_sem=edge_send,
+            recv_sem=halo_recv,
+            device_id={"dev": b - 1},
+            device_id_type=MESH,
+        )
+
+    for b in edges:
+        @pl.when(me != b - 1)
+        def _():
+            edge_copy(b).start()
+
+        @pl.when(me == b - 1)
+        def _():
+            for c in range(channels):
+                halo[c, me] = send[c, b * tiles]
 
     @pl.loop(1, tiles)
     def _(i):
@@ -164,7 +190,7 @@
 
         @pl.loop(1, n)
         def _(j):
-            tile_copy(t, lax.rem(me + j, n)).start()
+            tile_copy(t, peer_of(j)).start()
 
         for c in range(channels):
             recv[t, c, me] = send[c, me * tiles + t]
@@ -188,7 +214,7 @@
         for c in range(channels):
             dop[c, pl.ds(first, count), :] = result[c * count : (c + 1) * count]
 
-    def focus_rows(first, start, stop):
+    def focus_rows(into, first, start, stop):
         @pl.loop(start, stop)
         def _(step):
             row = pl.multiple_of(step * 16, 16)
@@ -216,11 +242,11 @@
                         new_imag = cre * im + cim * re
                         real = new_real if d == 0 else real + new_real
                         imag = new_imag if d == 0 else imag + new_imag
-                    foc[c, pl.ds(row, 16), at] = real.astype(BF16)
-                    foc[c, pl.ds(row, 16), wide + f * LANES : wide + (f + 1) * LANES] = imag.astype(BF16)
-
-    def image(slot, count):
-        columns = foc[:, :count, :].reshape(channels * count, 2 * wide)
+                    into[c, pl.ds(row, 16), at] = real.astype(BF16)
+                    into[c, pl.ds(row, 16), wide + f * LANES : wide + (f + 1) * LANES] = imag.astype(BF16)
+
+    def image(source, slot, count):
+        columns = source[:, :count, :].reshape(channels * count, 2 * wide)
         result = lax.dot_general(
             back_ref[...], columns, (((1,), (1,)), ((), ())), preferred_element_type=F32
         ).astype(BF16)
@@ -255,23 +281,31 @@
         device_id_type=MESH,
     )
 
-    @pl.when(me > 0)
+    at_edge = lax.rem(me, PLANE) == 0
+    before_edge = jnp.logical_or(lax.rem(me + 1, PLANE) == 0, me == n - 1)
+
+    @pl.when(jnp.logical_not(at_edge))
     def _():
         halo_copy.start()
 
     spectra(lambda c: recv[0, c], 0, LANES)
-
-    @pl.when(me < n - 1)
+    focus_rows(early, 0, 0, LANES // 16 - 1)
+
+    @pl.when(jnp.logical_not(before_edge))
     def _():
         halo_copy.wait_recv()
+
+    @pl.when(jnp.logical_and(before_edge, me < n - 1))
+    def _():
+        wait_bytes(halo_recv, halo.at[:, : n - 1])
 
     @pl.when(me == n - 1)
     def _():
         halo[...] = jnp.zeros_like(halo)
 
     spectra(lambda c: halo[c], block, MARG)
-    focus_rows(block, 0, MARG // 16)
-    image(tiles, MARG)
+    focus_rows(foc, block, 0, MARG // 16)
+    image(foc, tiles, MARG)
 
     @pl.loop(1, tiles)
     def _(i):
@@ -279,19 +313,24 @@
         wait_bytes(tile_sem.at[t], recv.at[t, :, : n - 1])
         first = pl.multiple_of(t * LANES, LANES)
         spectra(lambda c: recv[t, c], first, LANES)
-        focus_rows(first, 0, LANES // 16)
-        image(t, LANES)
+        focus_rows(foc, first, 0, LANES // 16)
+        image(foc, t, LANES)
         pick(t)
 
-    focus_rows(0, 0, LANES // 16)
-    image(0, LANES)
+    focus_rows(early, 0, LANES // 16 - 1, LANES // 16)
+    image(early, 0, LANES)
     pick(0)
 
     wait_bytes(send_sem, send.at[:, : (n - 1) * tiles])
 
-    @pl.when(me > 0)
+    @pl.when(jnp.logical_not(at_edge))
     def _():
         halo_copy.wait_send()
+
+    for b in edges:
+        @pl.when(me != b - 1)
+        def _():
+            edge_copy(b).wait_send()
 
 
 def body(echoes, range_phase, offsets, tap_weights, channel_mix, azimuth_filter):
@@ -313,7 +352,7 @@
     rows = 2 * pulses
     vmem = pl.BlockSpec(memory_space=pltpu.VMEM)
     call = pl.pallas_call(
-        functools.partial(kernel, n, pulses, wide, tiles),
+        functools.partial(kernel, n, pulses, wide, tiles, tuple(range(PLANE, n, PLANE))),
         out_shape=jax.ShapeDtypeStruct((2, channels, group_pulses, block), BF16),
         in_specs=[vmem] * 10,
         out_specs=vmem,
@@ -327,12 +366,14 @@
             pltpu.VMEM((channels, n, rows, LANES), BF16),
             pltpu.VMEM((channels, block + MARG + 16, 2 * wide), F32),
             pltpu.VMEM((channels, LANES, 2 * wide), BF16),
+            pltpu.VMEM((channels, LANES, 2 * wide), BF16),
             pltpu.VMEM((tiles + 1, channels, 2 * group_pulses, LANES), BF16),
             pltpu.VMEM((2, R1, LANES), F32),
             pltpu.VMEM((2, channels, channels, wide), F32),
             pltpu.SemaphoreType.DMA,
             pltpu.SemaphoreType.DMA,
             pltpu.SemaphoreType.DMA((tiles,)),
+            pltpu.SemaphoreType.DMA,
             pltpu.SemaphoreType.DMA,
             pltpu.SemaphoreType.DMA,
         ],

time: 84.3 us -> 67.4 us (0.80)
  the two profiles are of different devices: /device:TPU:15 before, /device:TPU:0 now
where the time goes in v2:
time: 67.4 us; the launch traced here: 67.3 us
  Pallas kernels  64.2 us (95%)
  local copies, waits for them, and re-layouts  3.05 us (5%)
    pallas_call x1, Pallas kernels, body(): call(echoes, range_phase.reshape(R1, range_bins // R1), offsets.reshape(t...  64.2 us
    unnamed x1, local copies, waits for them, and re-layouts  3.05 us

profile of v2, /device:TPU:0, one launch (start us, length us, event | category | flops | bytes accessed | tf_op | source)
XLA Modules:
  0.0 67.3 jit_solution(14720181410963645992)
XLA Ops:
  0.0 64.2 %focus.1 = bf16[2,4,256,512]{3,2,1,0:T(8,128)(2,1)} custom-call(bf16[2,4,8,16384]{3,2,1,0:T(8,128)(2,1)} %echo_ref.1, f32[128,128]{1,0:T(8,128)} %bitcast.2, s32[4,128]{1,0:T(4,128)} %bitcast.3, f32[8,384]{1,0:T(8,128)} %taps_ref.1, f32[2,4,4,384]{3,2,1,0:T(4,128)} %mix_ref.1, f32[2,4,384]{2,1,0:T(4,128)} %filt_ref.1, ...), custom_call_target="tpu_custom_call" | custom-call | flops 6000000000 | bytes 8388608 | tf_op jit(solution)/shard_map/focus/pallas_call | solution.py:388
  64.3 3.0 %copy.12 = bf16[2,4,256,512]{3,2,1,0:T(8,128)(2,1)} copy(bf16[2,4,256,512]{3,2,1,0:T(8,128)(2,1)} %focus.1) | data formatting | bytes 4194304

commit v3 on v2

--- a/solution.py
+++ b/solution.py
@@ -13,6 +13,7 @@
 LANES = 128
 MARG = 64
 PLANE = 8
+SPAN = 120
 F32 = jnp.float32
 BF16 = jnp.bfloat16
 MESH = pl.DeviceIdType.MESH
@@ -24,14 +25,18 @@
     return np.cos(angle), np.sin(angle)
 
 
-def range_table():
-    index = np.arange(R1)
-    cosine, sine = phases(index, index, R1)
+def bin_order():
+    place = np.arange(R1)
+    return place // MARG * MARG + place % 8 * 8 + place % MARG // 8
+
+
+def range_table(order):
+    cosine, sine = phases(order, np.arange(R1), R1)
     return np.block([[cosine, -sine], [sine, cosine]]).astype(BF16)
 
 
-def twist_tables(range_bins):
-    cosine, sine = phases(np.arange(R1), np.arange(range_bins // R1), range_bins)
+def twist_tables(order, range_bins):
+    cosine, sine = phases(order, np.arange(range_bins // R1), range_bins)
     scale = 1.0 / math.sqrt(range_bins)
     return np.stack([cosine * scale, sine * scale]).astype(np.float32)
 
@@ -66,7 +71,7 @@
 def kernel(
     n, pulses, wide, tiles, edges,
     echo_ref, phase_ref, offs_ref, taps_ref, mix_ref, filt_ref,
-    rng_ref, twist_ref, fwd_ref, back_ref,
+    first_ref, second_ref, twist_ref, fwd_ref, back_ref,
     out_ref,
     raw, spec, part, comp, send, recv, halo, dop, foc, early, img, phase, coef,
     send_sem, first_sem, tile_sem, halo_send, halo_recv, edge_send,
@@ -112,7 +117,7 @@
         half = 4
         for q0 in range(0, pulses, half):
             span = slice(q0 * LANES, (q0 + half) * LANES)
-            section = jnp.dot(rng_ref[...], spec[:, span], preferred_element_type=F32)
+            section = jnp.dot(first_ref[...], spec[:, span], preferred_element_type=F32)
             for q in range(half):
                 real = section[:R1, q * LANES : (q + 1) * LANES]
                 imag = section[R1:, q * LANES : (q + 1) * LANES]
@@ -120,7 +125,7 @@
                 part[at, :LANES] = (real * twist_ref[0] - imag * twist_ref[1]).astype(BF16)
                 part[at, LANES:] = (real * twist_ref[1] + imag * twist_ref[0]).astype(BF16)
             result = lax.dot_general(
-                rng_ref[...], part[span, :], (((1,), (1,)), ((), ())), preferred_element_type=F32
+                second_ref[...], part[span, :], (((1,), (1,)), ((), ())), preferred_element_type=F32
             )
             for q in range(half):
                 at = slice(q * LANES, (q + 1) * LANES)
@@ -212,14 +217,28 @@
             window, fwd_ref[...], (((0,), (0,)), ((), ())), preferred_element_type=F32
         ).astype(BF16).astype(F32)
         for c in range(channels):
-            dop[c, pl.ds(first, count), :] = result[c * count : (c + 1) * count]
+            for h in range(count // MARG):
+                at = pl.multiple_of((first + h) * SPAN, 8)
+                start = c * count + h * MARG
+                dop[c, pl.ds(at, MARG), :] = result[start : start + MARG]
+
+    def extend(b):
+        here = dop.at[:, pl.ds(pl.multiple_of(b * SPAN, 8), SPAN), :]
+        after = dop.at[:, pl.ds(pl.multiple_of((b + 1) * SPAN, 8), MARG), :]
+        top = lax.broadcasted_iota(jnp.int32, (8, 2 * wide), 0) == 0
+        for c in range(channels):
+            for m in range(taps - 1):
+                rows_here = slice(m * 8, m * 8 + 8)
+                mixed = jnp.where(top, after[c, rows_here, :], here[c, rows_here, :])
+                here[c, MARG + m * 8 : MARG + m * 8 + 8, :] = pltpu.roll(mixed, 7, 0)
 
     def focus_rows(into, first, start, stop):
         @pl.loop(start, stop)
         def _(step):
             row = pl.multiple_of(step * 16, 16)
-            base = pl.multiple_of(first + row, 16)
-            near = dop.at[:, pl.ds(base, 24), :]
+            part_of = step // 4
+            base = pl.multiple_of((first + part_of) * SPAN + (step - part_of * 4) * 16, 8)
+            near = dop.at[:, pl.ds(base, 16 + 8 * (taps - 1)), :]
             for f in range(wide // LANES):
                 at = slice(f * LANES, (f + 1) * LANES)
                 moved = []
@@ -229,7 +248,7 @@
                         where = slice(ri * wide + f * LANES, ri * wide + (f + 1) * LANES)
                         total = near[d, :16, where] * taps_ref[0:1, at]
                         for j in range(1, taps):
-                            total = total + near[d, j : j + 16, where] * taps_ref[j : j + 1, at]
+                            total = total + near[d, 8 * j : 8 * j + 16, where] * taps_ref[j : j + 1, at]
                         pair.append(total)
                     moved.append(pair)
                 for c in range(channels):
@@ -255,7 +274,8 @@
 
     def pick(t):
         target = offs_ref[pl.ds(t, 1), :] + lax.broadcasted_iota(jnp.int32, (1, LANES), 1)
-        source = lax.broadcasted_iota(jnp.int32, (2 * LANES, LANES), 0)
+        place = lax.broadcasted_iota(jnp.int32, (2 * LANES, LANES), 0)
+        source = (place >> 6 << 6) + ((place & 7) << 3) + (place >> 3 & 7)
         onehot = jnp.where(source == target, 1.0, 0.0).astype(BF16)
         for c in range(channels):
             both = jnp.concatenate([img[t, c], img[t + 1, c]], axis=1)
@@ -269,7 +289,9 @@
         pltpu.make_async_copy(ref, ref, sem).wait()
 
     wait_bytes(first_sem, recv.at[0, :, : n - 1])
-    dop[:, block + MARG :, :] = jnp.zeros_like(dop[:, block + MARG :, :])
+    last = block // MARG
+    end = (last + 1) * SPAN
+    dop[:, end:, :] = jnp.zeros_like(dop[:, end:, :])
     img[tiles, :, :, MARG:] = jnp.zeros_like(img[tiles, :, :, MARG:])
 
     halo_copy = pltpu.make_async_remote_copy(
@@ -289,7 +311,8 @@
         halo_copy.start()
 
     spectra(lambda c: recv[0, c], 0, LANES)
-    focus_rows(early, 0, 0, LANES // 16 - 1)
+    extend(0)
+    focus_rows(early, 0, 0, 4)
 
     @pl.when(jnp.logical_not(before_edge))
     def _():
@@ -303,21 +326,25 @@
     def _():
         halo[...] = jnp.zeros_like(halo)
 
-    spectra(lambda c: halo[c], block, MARG)
-    focus_rows(foc, block, 0, MARG // 16)
+    spectra(lambda c: halo[c], last, MARG)
+    extend(last)
+    focus_rows(foc, last, 0, MARG // 16)
     image(foc, tiles, MARG)
 
     @pl.loop(1, tiles)
     def _(i):
         t = tiles - i
         wait_bytes(tile_sem.at[t], recv.at[t, :, : n - 1])
-        first = pl.multiple_of(t * LANES, LANES)
+        first = t * (LANES // MARG)
         spectra(lambda c: recv[t, c], first, LANES)
+        extend(first)
+        extend(first + 1)
         focus_rows(foc, first, 0, LANES // 16)
         image(foc, t, LANES)
         pick(t)
 
-    focus_rows(early, 0, LANES // 16 - 1, LANES // 16)
+    extend(1)
+    focus_rows(early, 0, 4, 8)
     image(early, 0, LANES)
     pick(0)
 
@@ -354,7 +381,7 @@
     call = pl.pallas_call(
         functools.partial(kernel, n, pulses, wide, tiles, tuple(range(PLANE, n, PLANE))),
         out_shape=jax.ShapeDtypeStruct((2, channels, group_pulses, block), BF16),
-        in_specs=[vmem] * 10,
+        in_specs=[vmem] * 11,
         out_specs=vmem,
         scratch_shapes=[
             pltpu.VMEM((2, R1 * pulses, LANES), F32),
@@ -364,7 +391,7 @@
             pltpu.VMEM((channels, R1, rows, LANES), BF16),
             pltpu.VMEM((tiles, channels, n, rows, LANES), BF16),
             pltpu.VMEM((channels, n, rows, LANES), BF16),
-            pltpu.VMEM((channels, block + MARG + 16, 2 * wide), F32),
+            pltpu.VMEM((channels, (block // MARG + 1) * SPAN + MARG, 2 * wide), F32),
             pltpu.VMEM((channels, LANES, 2 * wide), BF16),
             pltpu.VMEM((channels, LANES, 2 * wide), BF16),
             pltpu.VMEM((tiles + 1, channels, 2 * group_pulses, LANES), BF16),
@@ -378,7 +405,7 @@
             pltpu.SemaphoreType.DMA,
         ],
         compiler_params=pltpu.CompilerParams(
-            collective_id=0, has_side_effects=True, vmem_limit_bytes=56 * 1024 * 1024
+            collective_id=0, has_side_effects=True, vmem_limit_bytes=36 * 1024 * 1024
         ),
         cost_estimate=pl.CostEstimate(
             flops=6 * 10**9, bytes_accessed=8 * 2**20, transcendentals=0
@@ -392,8 +419,9 @@
         tap_weights,
         channel_mix,
         azimuth_filter,
-        jnp.asarray(range_table()),
-        jnp.asarray(twist_tables(range_bins)),
+        jnp.asarray(range_table(bin_order())),
+        jnp.asarray(range_table(np.arange(R1))),
+        jnp.asarray(twist_tables(bin_order(), range_bins)),
         jnp.asarray(doppler_table(pulse_of_row, wide)),
         jnp.asarray(image_table(group_pulses, wide)),
     )

time: 67.4 us -> 72.7 us (1.079)
  local copies, waits for them, and re-layouts: 3.05 us -> 11.6 us
  Pallas kernels: 64.2 us -> 60.6 us
    unnamed x1 -> x23, local copies, waits for them, and re-layouts: 3.05 us -> 11.6 us
    pallas_call x1, Pallas kernels: 64.2 us -> 60.6 us  [body(): call(echoes, range_phase.reshape(R1, range_bins // R1), offsets.reshape(t...]
where the time goes in v3:
time: 72.7 us; the launch traced here: 72.2 us
  Pallas kernels  60.6 us (83%)
  local copies, waits for them, and re-layouts  11.6 us (16%)
    pallas_call x1, Pallas kernels, body(): call(echoes, range_phase.reshape(R1, range_bins // R1), offsets.reshape(t...  60.6 us
    unnamed x23, local copies, waits for them, and re-layouts  11.6 us

profile of v3, /device:TPU:0, one launch (start us, length us, event | category | flops | bytes accessed | tf_op | source)
XLA Modules:
  0.0 72.2 jit_solution(116025961156487644)
XLA Ops:
  0.0 0.0 copy-start
  0.0 1.6 %copy-done = bf16[2,4,8,16384]{3,2,1,0:T(8,128)(2,1)S(1)} copy-done((bf16[2,4,8,16384]{3,2,1,0:T(8,128)(2,1)S(1)}, bf16[2,4,8,16384]{3,2,1,0:T(8,128)(2,1)}, u32[]{:S(2)}) %copy-start) | copy-done | bytes 2097176
  1.6 0.0 copy-start.1
  1.6 0.8 %copy-done.1 = f32[16384]{0:T(1024)S(1)} copy-done((f32[16384]{0:T(1024)S(1)}, f32[16384]{0:T(1024)}, u32[]{:S(2)}) %copy-start.1) | copy-done | bytes 65560
  2.4 0.0 copy-start.2
  2.4 0.8 %copy-done.2 = f32[2,4,4,384]{3,2,1,0:T(4,128)S(1)} copy-done((f32[2,4,4,384]{3,2,1,0:T(4,128)S(1)}, f32[2,4,4,384]{3,2,1,0:T(4,128)}, u32[]{:S(2)}) %copy-start.2) | copy-done | bytes 49176
  3.2 0.0 copy-start.3
  3.2 0.7 copy-done.3
  3.9 0.0 copy-start.4
  3.9 0.7 copy-done.4
  4.6 0.0 copy-start.5
  4.6 0.7 copy-done.5
  5.3 0.0 copy-start.6
  5.3 1.1 %copy-done.6 = bf16[512,768]{1,0:T(8,128)(2,1)S(1)} copy-done((bf16[512,768]{1,0:T(8,128)(2,1)S(1)}, bf16[512,768]{1,0:T(8,128)(2,1)}, u32[]{:S(2)}) %copy-start.6) | copy-done | bytes 786456
  6.5 0.0 copy-start.7
  6.5 1.1 %copy-done.7 = bf16[512,768]{1,0:T(8,128)(2,1)S(1)} copy-done((bf16[512,768]{1,0:T(8,128)(2,1)S(1)}, bf16[512,768]{1,0:T(8,128)(2,1)}, u32[]{:S(2)}) %copy-start.7) | copy-done | bytes 786456
  7.6 0.0 copy-start.8
  7.6 0.9 %copy-done.8 = f32[2,128,128]{2,1,0:T(8,128)S(1)} copy-done((f32[2,128,128]{2,1,0:T(8,128)S(1)}, f32[2,128,128]{2,1,0:T(8,128)}, u32[]{:S(2)}) %copy-start.8) | copy-done | bytes 131096
  8.5 0.0 copy-start.9
  8.5 0.9 %copy-done.9 = bf16[256,256]{1,0:T(8,128)(2,1)S(1)} copy-done((bf16[256,256]{1,0:T(8,128)(2,1)S(1)}, bf16[256,256]{1,0:T(8,128)(2,1)}, u32[]{:S(2)}) %copy-start.9) | copy-done | bytes 131096
  9.4 0.0 copy-start.10
  9.4 0.9 %copy-done.10 = bf16[256,256]{1,0:T(8,128)(2,1)S(1)} copy-done((bf16[256,256]{1,0:T(8,128)(2,1)S(1)}, bf16[256,256]{1,0:T(8,128)(2,1)}, u32[]{:S(2)}) %copy-start.10) | copy-done | bytes 131096
  10.3 60.6 %focus.1 = bf16[2,4,256,512]{3,2,1,0:T(8,128)(2,1)S(1)} custom-call(bf16[2,4,8,16384]{3,2,1,0:T(8,128)(2,1)S(1)} %copy-done, f32[128,128]{1,0:T(8,128)S(1)} %bitcast.2, s32[4,128]{1,0:T(4,128)S(1)} %bitcast.3, f32[8,384]{1,0:T(8,128)S(1)} %copy-done.3, f32[2,4,4,384]{3,2,1,0:T(4,128)S(1)} %copy-done.2, f32[2,4,384]{2,1,0:T(4,128)S(1)} %copy-done.4, ...), custom_call_target="tpu_custom_call" | custom-call | flops 6000000000 | bytes 8388608 | tf_op jit(solution)/shard_map/focus/pallas_call | solution.py:415
  70.9 1.3 %copy.13 = bf16[2,4,256,512]{3,2,1,0:T(8,128)(2,1)} copy(bf16[2,4,256,512]{3,2,1,0:T(8,128)(2,1)S(1)} %focus.1) | data formatting | bytes 4194304
Async XLA Ops:
  0.0 1.6 %copy-start = (bf16[2,4,8,16384]{3,2,1,0:T(8,128)(2,1)S(1)}, bf16[2,4,8,16384]{3,2,1,0:T(8,128)(2,1)}, u32[]{:S(2)}) copy-start(bf16[2,4,8,16384]{3,2,1,0:T(8,128)(2,1)} %echo_ref.1) | copy-start | bytes 6291460
  1.6 0.8 %copy-start.1 = (f32[16384]{0:T(1024)S(1)}, f32[16384]{0:T(1024)}, u32[]{:S(2)}) copy-start(f32[16384]{0:T(1024)} %param.12) | copy-start | bytes 196612
  2.4 0.8 %copy-start.2 = (f32[2,4,4,384]{3,2,1,0:T(4,128)S(1)}, f32[2,4,4,384]{3,2,1,0:T(4,128)}, u32[]{:S(2)}) copy-start(f32[2,4,4,384]{3,2,1,0:T(4,128)} %mix_ref.1) | copy-start | bytes 147460
  3.2 0.7 copy-start.3
  3.9 0.7 copy-start.4
  4.6 0.7 copy-start.5
  5.3 1.1 %copy-start.6 = (bf16[512,768]{1,0:T(8,128)(2,1)S(1)}, bf16[512,768]{1,0:T(8,128)(2,1)}, u32[]{:S(2)}) copy-start(bf16[512,768]{1,0:T(8,128)(2,1)} %constant.14.clone.back_ref) | copy-start | bytes 2359300
  6.5 1.1 %copy-start.7 = (bf16[512,768]{1,0:T(8,128)(2,1)S(1)}, bf16[512,768]{1,0:T(8,128)(2,1)}, u32[]{:S(2)}) copy-start(bf16[512,768]{1,0:T(8,128)(2,1)} %constant.13.clone.fwd_ref) | copy-start | bytes 2359300
  7.6 0.9 %copy-start.8 = (f32[2,128,128]{2,1,0:T(8,128)S(1)}, f32[2,128,128]{2,1,0:T(8,128)}, u32[]{:S(2)}) copy-start(f32[2,128,128]{2,1,0:T(8,128)} %constant.12.clone.twist_ref) | copy-start | bytes 393220
  8.5 0.9 %copy-start.9 = (bf16[256,256]{1,0:T(8,128)(2,1)S(1)}, bf16[256,256]{1,0:T(8,128)(2,1)}, u32[]{:S(2)}) copy-start(bf16[256,256]{1,0:T(8,128)(2,1)} %constant.11.clone.second_ref) | copy-start | bytes 393220
  9.4 0.9 %copy-start.10 = (bf16[256,256]{1,0:T(8,128)(2,1)S(1)}, bf16[256,256]{1,0:T(8,128)(2,1)}, u32[]{:S(2)}) copy-start(bf16[256,256]{1,0:T(8,128)(2,1)} %constant.10.clone.first_ref) | copy-start | bytes 393220

commit v4 on v3

--- a/solution.py
+++ b/solution.py
@@ -70,12 +70,28 @@
 
 def kernel(
     n, pulses, wide, tiles, edges,
-    echo_ref, phase_ref, offs_ref, taps_ref, mix_ref, filt_ref,
-    first_ref, second_ref, twist_ref, fwd_ref, back_ref,
-    out_ref,
-    raw, spec, part, comp, send, recv, halo, dop, foc, early, img, phase, coef,
-    send_sem, first_sem, tile_sem, halo_send, halo_recv, edge_send,
+    *refs,
 ):
+    far, out_ref, held, rest = refs[:11], refs[11], refs[12:23], refs[23:]
+    echo_ref, phase_ref, offs_ref, taps_ref, mix_ref, filt_ref = held[:6]
+    first_ref, second_ref, twist_ref, fwd_ref, back_ref = held[6:]
+    raw, spec, part, comp, send, recv, halo, dop, foc, early, img, phase, coef = rest[:13]
+    send_sem, first_sem, tile_sem, halo_send, halo_recv, edge_send, echo_sem, load_sem = rest[13:]
+
+    def load_echo(c):
+        return pltpu.make_async_copy(far[0].at[:, c], held[0].at[:, c], echo_sem.at[c])
+
+    def load(k):
+        return pltpu.make_async_copy(far[k], held[k], load_sem.at[k])
+
+    load(1).start()
+    load_echo(0).start()
+    for k in (6, 8, 7):
+        load(k).start()
+    for c in range(1, echo_ref.shape[1]):
+        load_echo(c).start()
+    for k in (9, 3, 4, 5, 10, 2):
+        load(k).start()
     me = lax.axis_index("dev")
     channels = echo_ref.shape[1]
     taps = taps_ref.shape[0]
@@ -96,9 +112,12 @@
             barrier, inc=1, device_id={"dev": lax.rem(me + i, n)}, device_id_type=MESH
         )
 
+    load(1).wait()
     cosine, sine = cos_sin(phase_ref[...])
     phase[0] = cosine
     phase[1] = sine
+    for k in (6, 7, 8):
+        load(k).wait()
 
     def range_channel(c):
         for ri in range(2):
@@ -157,6 +176,7 @@
 
     @pl.loop(0, channels)
     def _(c):
+        load_echo(c).wait()
         range_channel(c)
 
         @pl.when(c == 0)
@@ -199,6 +219,9 @@
 
         for c in range(channels):
             recv[t, c, me] = send[c, me * tiles + t]
+
+    for k in (9, 3, 4, 5, 10, 2):
+        load(k).wait()
 
     for c in range(channels):
         for ri in range(2):
@@ -378,12 +401,26 @@
     pulses = echoes.shape[2]
     rows = 2 * pulses
     vmem = pl.BlockSpec(memory_space=pltpu.VMEM)
+    operands = (
+        echoes,
+        range_phase.reshape(R1, range_bins // R1),
+        offsets.reshape(tiles, LANES),
+        tap_weights,
+        channel_mix,
+        azimuth_filter,
+        jnp.asarray(range_table(bin_order())),
+        jnp.asarray(range_table(np.arange(R1))),
+        jnp.asarray(twist_tables(bin_order(), range_bins)),
+        jnp.asarray(doppler_table(pulse_of_row, wide)),
+        jnp.asarray(image_table(group_pulses, wide)),
+    )
     call = pl.pallas_call(
         functools.partial(kernel, n, pulses, wide, tiles, tuple(range(PLANE, n, PLANE))),
         out_shape=jax.ShapeDtypeStruct((2, channels, group_pulses, block), BF16),
-        in_specs=[vmem] * 11,
+        in_specs=[pl.BlockSpec(memory_space=pltpu.HBM)] * 11,
         out_specs=vmem,
-        scratch_shapes=[
+        scratch_shapes=[pltpu.VMEM(a.shape, a.dtype) for a in operands]
+        + [
             pltpu.VMEM((2, R1 * pulses, LANES), F32),
             pltpu.VMEM((2 * R1, pulses * LANES), BF16),
             pltpu.VMEM((pulses * LANES, 2 * LANES), BF16),
@@ -403,28 +440,18 @@
             pltpu.SemaphoreType.DMA,
             pltpu.SemaphoreType.DMA,
             pltpu.SemaphoreType.DMA,
+            pltpu.SemaphoreType.DMA((channels,)),
+            pltpu.SemaphoreType.DMA((11,)),
         ],
         compiler_params=pltpu.CompilerParams(
-            collective_id=0, has_side_effects=True, vmem_limit_bytes=36 * 1024 * 1024
+            collective_id=0, has_side_effects=True, vmem_limit_bytes=56 * 1024 * 1024
         ),
         cost_estimate=pl.CostEstimate(
             flops=6 * 10**9, bytes_accessed=8 * 2**20, transcendentals=0
         ),
         name="focus",
     )
-    return call(
-        echoes,
-        range_phase.reshape(R1, range_bins // R1),
-        offsets.reshape(tiles, LANES),
-        tap_weights,
-        channel_mix,
-        azimuth_filter,
-        jnp.asarray(range_table(bin_order())),
-        jnp.asarray(range_table(np.arange(R1))),
-        jnp.asarray(twist_tables(bin_order(), range_bins)),
-        jnp.asarray(doppler_table(pulse_of_row, wide)),
-        jnp.asarray(image_table(group_pulses, wide)),
-    )
+    return call(*operands)
 
 
 def solution(mesh):

time: 72.7 us -> 66.2 us (0.911)
  local copies, waits for them, and re-layouts: 11.6 us -> 3.05 us
  Pallas kernels: 60.6 us -> 63 us
    unnamed x23 -> x1, local copies, waits for them, and re-layouts: 11.6 us -> 3.05 us
    pallas_call x1, Pallas kernels: 60.6 us -> 63 us  [body(): return call(*operands)]
where the time goes in v4:
time: 66.2 us; the launch traced here: 66.1 us
  Pallas kernels  63 us (95%)
  local copies, waits for them, and re-layouts  3.05 us (5%)
    pallas_call x1, Pallas kernels, body(): return call(*operands)  63 us
    unnamed x1, local copies, waits for them, and re-layouts  3.05 us

profile of v4, /device:TPU:0, one launch (start us, length us, event | category | flops | bytes accessed | tf_op | source)
XLA Modules:
  0.0 66.1 jit_solution(8206704953786482288)
XLA Ops:
  0.0 63.0 %focus.1 = bf16[2,4,256,512]{3,2,1,0:T(8,128)(2,1)} custom-call(bf16[2,4,8,16384]{3,2,1,0:T(8,128)(2,1)} %refs_0_.1, f32[128,128]{1,0:T(8,128)} %bitcast.2, s32[4,128]{1,0:T(4,128)} %bitcast.3, f32[8,384]{1,0:T(8,128)} %refs_3_.1, f32[2,4,4,384]{3,2,1,0:T(4,128)} %refs_4_.1, f32[2,4,384]{2,1,0:T(4,128)} %refs_5_.1, bf16[256,256]{1,0:T(8,128)(2,1)} %constant.10.clone.refs_6_, ...), custom_call_target="tpu_custom_call" | custom-call | flops 6000000000 | bytes 8388608 | tf_op jit(solution)/shard_map/focus/pallas_call | solution.py:454
  63.0 3.0 %copy.13 = bf16[2,4,256,512]{3,2,1,0:T(8,128)(2,1)} copy(bf16[2,4,256,512]{3,2,1,0:T(8,128)(2,1)} %focus.1) | data formatting | bytes 4194304
